TPU v7x, 32 devices: a whole 2x2x4 slice. The times are simulated.
32 devices in a mesh: row: 4 (over y, x), col: 8 (over z, core).
Axes of the slice: x: 2, y: 2, z: 4, core: 2. Of those that a mesh axis runs over, the one named last changes fastest.
Arguments:
- points: float32 [4096, 128], P(('row', 'col')), may hold values from -4 to 4
- labels: int32 [4096], P(('row', 'col')), may hold values from 0 to 63
- coefficients: float32 [4096, 64], P(('row', 'col')), as said below
Outputs:
- new_coefficients: float32 [4096, 64], P(('row', 'col'))
- probabilities: float32 [4096, 64], P(('row', 'col'))
Inputs may be any that keep to these rules, and one draw needn't show every extreme that they name: `coefficients`: entries have magnitude at most 300 * sqrt(4096) / 16.
All inputs are finite; a program needn't handle non-finite values.
Results may differ from a plain program's by a relative error of at most 0.012.
The roundings to bfloat16 on the way count: a program that leaves them out, or rounds other values in their place, can miss the bound.
Values may be sent and summed in bfloat16 or wider, within the bound.
A program may use at most 64 MiB of HBM per device.

v0:
```python
import math

import jax
import jax.numpy as jnp
from jax import lax
from jax.sharding import PartitionSpec as P

FEAT = 128
CLASSES = 64


def pair_tile(left_points, right_points, right_squares):
    left_squares = jnp.sum(left_points * left_points, axis=1)
    products = lax.dot_general(
        left_points,
        right_points,
        (((1,), (1,)), ((), ())),
        precision=lax.Precision.HIGHEST,
        preferred_element_type=jnp.float32,
    )
    distance = left_squares[:, None] + right_squares[None, :] - 2.0 * products
    return jnp.exp(-distance / FEAT).astype(jnp.bfloat16)


def on_device(points, labels, coefficients):
    owned_rows = points.shape[0]
    row_count = lax.axis_size("row")
    col_count = lax.axis_size("col")
    total_points = owned_rows * row_count * col_count
    logit_scale = 16.0 / math.sqrt(total_points)
    column_points = lax.all_gather(points, "row", axis=0, tiled=True)
    column_squares = jnp.sum(column_points * column_points, axis=1)
    kernel_tile = pair_tile(
        lax.all_gather(points, "col", axis=0, tiled=True), column_points, column_squares
    )

    def kernel_apply(current):
        rounded = current.astype(jnp.bfloat16)
        row_values = lax.all_gather(rounded, "col", axis=0, tiled=True)
        return lax.psum_scatter(
            lax.dot_general(
                kernel_tile,
                row_values,
                (((0,), (0,)), ((), ())),
                preferred_element_type=jnp.float32,
            ),
            "row",
            scatter_dimension=0,
            tiled=True,
        )

    onehot = (labels[:, None] == jnp.arange(CLASSES, dtype=jnp.int32)[None, :]).astype(jnp.float32)
    current = coefficients
    logits = logit_scale * kernel_apply(current)
    probabilities = jax.nn.softmax(logits, axis=1)
    residual = logit_scale * (probabilities - onehot)
    current = current - kernel_apply(residual)
    return (current, probabilities)


def solution(mesh):
    return jax.shard_map(
        on_device,
        mesh=mesh,
        in_specs=(P(("row", "col"), None), P(("row", "col")), P(("row", "col"), None)),
        out_specs=(P(("row", "col"), None), P(("row", "col"), None)),
        check_vma=False,
    )
```

profile of v0, /device:TPU:0, one launch (start us, length us, event | category | flops | bytes accessed | tf_op | source)
XLA Modules:
  0.0 120.2 jit_solution(3269733011568141187)
XLA Ops:
  7.2 0.0 copy-start
  7.2 0.0 reduce-scatter.3.cloned.1.call-start
  7.2 16.8 %all_gather.12 = f32[1024,128]{1,0:T(8,128)S(1)} all-gather(f32[128,128]{1,0:T(8,128)} %param.3), channel_id=1, replica_groups=mesh['row'=4,'col'=8] {'col'}, dimensions={0}, use_global_device_ids=true | all-gather | bytes 589824 | tf_op jit(solution)/shard_map/all_gather | solution.py:34
  24.0 9.3 %all_gather.13 = f32[512,128]{1,0:T(8,128)S(1)} all-gather(f32[128,128]{1,0:T(8,128)} %param.3), channel_id=1, replica_groups=mesh['row'=4,'col'=8] {'row'}, dimensions={0}, use_global_device_ids=true | all-gather | bytes 327680 | tf_op jit(solution)/shard_map/all_gather | solution.py:31
  33.3 0.2 multiply_reduce_fusion
  33.5 0.1 multiply_reduce_fusion.1
  33.6 0.0 copy-done
  33.7 12.8 %all_gather.14 = bf16[1024,64]{0,1:T(8,128)(2,1)S(1)} all-gather(bf16[128,64]{0,1:T(8,128)(2,1)S(1)} %convert_element_type.13), channel_id=1, replica_groups=mesh['row'=4,'col'=8] {'col'}, dimensions={0}, use_global_device_ids=true | all-gather | bytes 147456 | tf_op jit(solution)/shard_map/all_gather | solution.py:39
  46.5 2.1 %exponential_convert_fusion = bf16[1024,512]{1,0:T(8,128)(2,1)S(1)} fusion(f32[1024,128]{1,0:T(8,128)S(1)} %all_gather.12, f32[512,128]{1,0:T(8,128)S(1)} %all_gather.13, f32[512]{0:T(512)S(1)} %multiply_reduce_fusion.1, f32[1024]{0:T(1024)S(1)} %multiply_reduce_fusion), kind=kOutput, calls=%fused_computation | convolution fusion | flops 808452096 | bytes 1841152 | tf_op jit(solution)/shard_map/dot_general | solution.py:14
  48.6 0.0 copy-start.1
  48.6 0.9 fusion.3
  49.6 0.0 reduce-scatter.3.cloned.1.call-update
  49.6 0.0 reduce-scatter.5.cloned.1.call-start
  49.6 22.8 %reduce-scatter.3.cloned.1.call-done = f32[128,64]{0,1:T(8,128)} async-done(((f32[512,64]{0,1:T(8,128)}), f32[128,64]{0,1:T(8,128)}) %reduce-scatter.3.cloned.1.call-update) | async-done | bytes 32784 | tf_op jit(solution)/shard_map/reduce_scatter | solution.py:40
  72.4 0.8 multiply_reduce_fusion.2
  73.2 0.8 fusion.1
  74.0 0.0 copy-done.1
  74.0 1.4 %multiply_convert_fusion = (bf16[128,64]{0,1:T(8,128)(2,1)S(1)}, f32[128,64]{0,1:T(8,128)}) fusion(s32[128]{0:T(128)S(1)} %copy-done.1, f32[128]{0:T(128)S(1)} %fusion.1, f32[128]{0:T(128)S(1)} %multiply_reduce_fusion.2, f32[128,64]{0,1:T(8,128)} %reduce-scatter.3.cloned.1.call-done), kind=kLoop, calls=%fused_computation.3 | loop fusion | flops 65536 | bytes 83456 | tf_op jit(solution)/shard_map/convert_element_type | solution.py:38
  75.4 12.9 %all_gather.15 = bf16[1024,64]{0,1:T(8,128)(2,1)S(1)} all-gather(bf16[128,64]{0,1:T(8,128)(2,1)S(1)} %get-tuple-element.2), channel_id=1, replica_groups=mesh['row'=4,'col'=8] {'col'}, dimensions={0}, use_global_device_ids=true | all-gather | bytes 147456 | tf_op jit(solution)/shard_map/all_gather | solution.py:39
  88.2 0.9 fusion.4
  89.2 0.0 reduce-scatter.5.cloned.1.call-update
  89.2 22.8 %reduce-scatter.5.cloned.1.call-done = f32[128,64]{0,1:T(8,128)} async-done(((f32[512,64]{0,1:T(8,128)}), f32[128,64]{0,1:T(8,128)}) %reduce-scatter.5.cloned.1.call-update) | async-done | bytes 32784 | tf_op jit(solution)/shard_map/reduce_scatter | solution.py:40
  112.0 1.4 %sub.21 = f32[128,64]{0,1:T(8,128)} subtract(f32[128,64]{0,1:T(8,128)S(1)} %copy-done, f32[128,64]{0,1:T(8,128)} %reduce-scatter.5.cloned.1.call-done) | non-fusion elementwise | flops 8192 | bytes 98304 | tf_op jit(solution)/shard_map/sub | solution.py:57
  (1 shorter events, 0.0 us)
Async XLA Ops:
  7.2 26.5 %copy-start = (f32[128,64]{0,1:T(8,128)S(1)}, f32[128,64]{0,1:T(8,128)}, u32[]{:S(2)}) copy-start(f32[128,64]{0,1:T(8,128)} %param.5) | copy-start | bytes 98308
  7.2 65.2 %reduce-scatter.3.cloned.1.call-start = ((), (), s32[]{:S(2)}) async-start(), calls=%async_computation.2 | async-start | bytes 163840 | tf_op jit(solution)/shard_map/reduce_scatter | solution.py:40
  48.6 25.4 %copy-start.1 = (s32[128]{0:T(128)S(1)}, s32[128]{0:T(128)}, u32[]{:S(2)}) copy-start(s32[128]{0:T(128)} %param.4) | copy-start | bytes 1540
  49.6 62.4 %reduce-scatter.5.cloned.1.call-start = ((), (), s32[]{:S(2)}) async-start(), calls=%async_computation.3 | async-start | bytes 163840 | tf_op jit(solution)/shard_map/reduce_scatter | solution.py:40
Sparse Core Ops, SparseCore 0:
  49.7 22.6 reduce-scatter.2
  89.3 22.5 reduce-scatter.4
where the time goes:
time: 121 us; the launch traced here: 120 us
  blocking collectives  51.7 us (43%)
  waiting for transfers between devices  45.6 us (38%)
  between operations  14.1 us (12%)
  other arithmetic  4.7 us (4%)
  matrix products  3.98 us (3%)
    reduce_scatter x2, waiting for transfers between devices, kernel_apply(): lax.psum_scatter(lax.dot_general(kernel_tile, row_values, (((0,), (0,)),...  45.5 us
    all_gather x2, blocking collectives, kernel_apply(): row_values = lax.all_gather(rounded, 'col', axis=0, tiled=True)  25.7 us
    all_gather x1, blocking collectives, on_device(): lax.all_gather(points, 'col', axis=0, tiled=True)  16.8 us
    all_gather x1, blocking collectives, on_device(): column_points = lax.all_gather(points, 'row', axis=0, tiled=True)  9.27 us
  transfers between devices with their start and end apart: 2, of which 2 were waited for; matrix products, arithmetic and copies ran while one was open for 0% of the time, Pallas kernels for 0%

commit v1 on v0

v1 whole, which is shorter than its diff:
```python
import functools
import math

import jax
import jax.numpy as jnp
from jax import lax
from jax.experimental import pallas as pl
from jax.experimental.pallas import tpu as pltpu
from jax.sharding import PartitionSpec as P

MESH = pl.DeviceIdType.MESH
NT = (((1,), (1,)), ((), ()))
NN = (((1,), (0,)), ((), ()))
GATHER_PLANE = False


def split_bf16(x):
    hi = x.astype(jnp.bfloat16)
    lo = (x - hi.astype(jnp.float32)).astype(jnp.bfloat16)
    return hi, lo


def kernel(
    lines, planes, cores, logit_scale,
    points_ref, labels_ref, coef_ref,
    new_ref, prob_ref,
    line_pts, plane_pts, values, tile, partial, landed,
    line_send, line_recv, plane_send, plane_recv, value_send, value_recv, part_send, part_recv,
):
    own, feat = points_ref.shape
    classes = coef_ref.shape[0]
    row = lax.axis_index("row")
    col = lax.axis_index("col")
    my_line = col // cores
    my_plane = row * cores + col % cores

    def line_device(i):
        return (row, i * cores + col % cores)

    def plane_device(j):
        return (j // cores, my_line * cores + j % cores)

    if GATHER_PLANE:
        gathers, my_gather, gather_device, gather_pts = planes, my_plane, plane_device, plane_pts
        reduces, my_reduce, reduce_device, reduce_pts = lines, my_line, line_device, line_pts
    else:
        gathers, my_gather, gather_device, gather_pts = lines, my_line, line_device, line_pts
        reduces, my_reduce, reduce_device, reduce_pts = planes, my_plane, plane_device, plane_pts

    barrier = pltpu.get_barrier_semaphore()
    for k in range(1, lines):
        pl.semaphore_signal(
            barrier, inc=1, device_id=line_device(lax.rem(my_line + k, lines)), device_id_type=MESH
        )
    for k in range(1, planes):
        pl.semaphore_signal(
            barrier, inc=1, device_id=plane_device(lax.rem(my_plane + k, planes)), device_id_type=MESH
        )

    hi, lo = split_bf16(points_ref[...])
    line_pts[my_line, :, :feat] = hi
    line_pts[my_line, :, feat:] = lo
    plane_pts[my_plane, :, :feat] = hi
    plane_pts[my_plane, :, feat:] = lo
    values[0, my_gather] = coef_ref[...].astype(jnp.bfloat16)
    pl.semaphore_wait(barrier, lines + planes - 2)

    def push(src, dst, send, recv, device):
        copy = pltpu.make_async_remote_copy(
            src_ref=src, dst_ref=dst, send_sem=send, recv_sem=recv, device_id=device, device_id_type=MESH
        )
        copy.start()
        return copy

    def recv_wait(buf, sem):
        pltpu.make_async_copy(buf, buf, sem).wait()

    sent = []
    for k in range(1, lines):
        to = lax.rem(my_line + k, lines)
        sent.append(push(line_pts.at[my_line], line_pts.at[my_line], line_send.at[k], line_recv.at[my_line], line_device(to)))
    for k in range(1, planes):
        to = lax.rem(my_plane + k, planes)
        sent.append(push(plane_pts.at[my_plane], plane_pts.at[my_plane], plane_send.at[k], plane_recv.at[my_plane], plane_device(to)))

    def send_values(phase):
        for k in range(1, gathers):
            to = lax.rem(my_gather + k, gathers)
            sent.append(push(
                values.at[phase, my_gather], values.at[phase, my_gather],
                value_send.at[phase, k], value_recv.at[phase, my_gather], gather_device(to),
            ))

    send_values(0)

    def wait_block(group, buf, recv, me, count, k):
        at = lax.rem(me + count - k, count)
        recv_wait(buf.at[at], recv.at[at])
        return at

    reduce_recv = line_recv if GATHER_PLANE else plane_recv
    gather_recv = plane_recv if GATHER_PLANE else line_recv
    for k in range(1, reduces):
        wait_block("reduce", reduce_pts, reduce_recv, my_reduce, reduces, k)
    right = reduce_pts[...].reshape(reduces * own, 2 * feat)
    right_f32 = right[:, :feat].astype(jnp.float32) + right[:, feat:].astype(jnp.float32)
    sq_hi, sq_rest = split_bf16(right_f32 * right_f32)
    right_squares = lax.dot_general(
        jnp.ones((8, 2 * feat), jnp.bfloat16), jnp.concatenate([sq_hi, sq_rest], axis=1), NT,
        preferred_element_type=jnp.float32,
    )[:1]

    for k in range(gathers):
        if k == 0:
            at = my_gather
        else:
            at = wait_block("gather", gather_pts, gather_recv, my_gather, gathers, k)
        left = gather_pts[at]
        left_hi, left_lo = left[:, :feat], left[:, feat:]
        left_f32 = left_hi.astype(jnp.float32) + left_lo.astype(jnp.float32)
        left_squares = jnp.sum(left_f32 * left_f32, axis=1, keepdims=True)
        swapped = jnp.concatenate([left_lo, left_hi], axis=1)
        products = lax.dot_general(left, right, NT, preferred_element_type=jnp.float32)
        products += lax.dot_general(swapped, right, NT, preferred_element_type=jnp.float32)
        distance = left_squares + right_squares - 2.0 * products
        tile[at] = jnp.exp(distance * (-1.0 / feat)).astype(jnp.bfloat16)

    def apply(phase):
        for k in range(1, gathers):
            at = lax.rem(my_gather + gathers - k, gathers)
            recv_wait(values.at[phase, at], value_recv.at[phase, at])
        left = jnp.concatenate([values[phase, i] for i in range(gathers)], axis=1)
        result = lax.dot_general(
            left, tile[...].reshape(gathers * own, reduces * own), NN, preferred_element_type=jnp.float32
        )
        for j in range(reduces):
            partial[phase, j] = result[:, j * own : (j + 1) * own]
        for k in range(1, reduces):
            to = lax.rem(my_reduce + k, reduces)
            sent.append(push(
                partial.at[phase, to], landed.at[phase, my_reduce],
                part_send.at[phase, k], part_recv.at[phase, my_reduce], reduce_device(to),
            ))
        total = partial[phase, my_reduce]
        for k in range(1, reduces):
            at = lax.rem(my_reduce + reduces - k, reduces)
            recv_wait(landed.at[phase, at], part_recv.at[phase, at])
            total += landed[phase, at]
        return total

    logits = logit_scale * apply(0)
    weights = jnp.exp(logits - jnp.max(logits, axis=0, keepdims=True))
    probabilities = weights / jnp.sum(weights, axis=0, keepdims=True)
    onehot = (lax.broadcasted_iota(jnp.int32, (classes, own), 0) == labels_ref[...]).astype(jnp.float32)
    values[1, my_gather] = (logit_scale * (probabilities - onehot)).astype(jnp.bfloat16)
    send_values(1)
    prob_ref[...] = probabilities
    new_ref[...] = coef_ref[...] - apply(1)
    for copy in sent:
        copy.wait_send()


def solution(mesh):
    rows, cols = mesh.shape["row"], mesh.shape["col"]
    cores = 2 if cols % 2 == 0 else 1
    lines, planes = cols // cores, rows * cores
    gathers, reduces = (planes, lines) if GATHER_PLANE else (lines, planes)

    def on_device(points, labels, coefficients):
        own, feat = points.shape
        classes = coefficients.shape[1]
        logit_scale = 16.0 / math.sqrt(own * rows * cols)
        vmem = pl.BlockSpec(memory_space=pltpu.VMEM)
        new, prob = pl.pallas_call(
            functools.partial(kernel, lines, planes, cores, logit_scale),
            out_shape=[jax.ShapeDtypeStruct((classes, own), jnp.float32)] * 2,
            in_specs=[vmem] * 3,
            out_specs=[vmem] * 2,
            scratch_shapes=[
                pltpu.VMEM((lines, own, 2 * feat), jnp.bfloat16),
                pltpu.VMEM((planes, own, 2 * feat), jnp.bfloat16),
                pltpu.VMEM((2, gathers, classes, own), jnp.bfloat16),
                pltpu.VMEM((gathers, own, reduces * own), jnp.bfloat16),
                pltpu.VMEM((2, reduces, classes, own), jnp.float32),
                pltpu.VMEM((2, reduces, classes, own), jnp.float32),
                pltpu.SemaphoreType.DMA((lines,)),
                pltpu.SemaphoreType.DMA((lines,)),
                pltpu.SemaphoreType.DMA((planes,)),
                pltpu.SemaphoreType.DMA((planes,)),
                pltpu.SemaphoreType.DMA((2, gathers)),
                pltpu.SemaphoreType.DMA((2, gathers)),
                pltpu.SemaphoreType.DMA((2, reduces)),
                pltpu.SemaphoreType.DMA((2, reduces)),
            ],
            compiler_params=pltpu.CompilerParams(
                collective_id=0, has_side_effects=True, vmem_limit_bytes=48 * 1024 * 1024
            ),
        )(points, labels.reshape(1, own), coefficients.T)
        return new.T, prob.T

    return jax.shard_map(
        on_device,
        mesh=mesh,
        in_specs=(P(("row", "col"), None), P(("row", "col")), P(("row", "col"), None)),
        out_specs=(P(("row", "col"), None), P(("row", "col"), None)),
        check_vma=False,
    )
```

time: 121 us -> 33.1 us (0.27)
  blocking collectives: 51.7 us -> 0 us
  waiting for transfers between devices: 45.6 us -> 0 us
  Pallas kernels: 0 us -> 28.8 us
  between operations: 14.1 us -> 0.65 us
  other arithmetic: 4.7 us -> 0 us
  matrix products: 3.98 us -> 0 us
  local copies, waits for them, and re-layouts: 0.01 us -> 3.48 us
    all_gather x4 -> x0, blocking collectives: 51.7 us -> none  [the longest x2 25.7 us: kernel_apply(): row_values = lax.all_gather(rounded, 'col', axis=0, tiled=True)]
    reduce_scatter x2 -> x0, waiting for transfers between devices: 45.5 us -> none  [kernel_apply(): lax.psum_scatter(lax.dot_general(kernel_tile, row_values, (((0,), (0,)),...]
    pallas_call x0 -> x1, Pallas kernels: none -> 28.8 us  [on_device(): pl.pallas_call(functools.partial(kernel, lines, planes, cores, logit_scal...]
    dot_general x3 -> x0, matrix products: 3.98 us -> none  [the longest x1 2.11 us: pair_tile(): lax.dot_general(left_points, right_points, (((1,), (1,)), ((), ())), prec...]
    unnamed x4 -> x8, local copies, waits for them, and re-layouts: 0.01 us -> 3.48 us
    convert_element_type x2 -> x0, other arithmetic: 1.4 us -> none  [kernel_apply(): rounded = current.astype(jnp.bfloat16)]
    sub x1 -> x0, other arithmetic: 1.38 us -> none  [on_device(): current = current - kernel_apply(residual)]
  transfers between devices with their start and end apart: 2 -> 0, of which waited for: 2 -> 0; matrix products, arithmetic and copies ran while one was open for 0% -> 0% of each run, Pallas kernels for 0% -> 0%
where the time goes in v1:
time: 33.1 us; the launch traced here: 32.9 us
  Pallas kernels  28.8 us (87%)
  local copies, waits for them, and re-layouts  3.48 us (11%)
  between operations  0.65 us (2%)
    pallas_call x1, Pallas kernels, on_device(): pl.pallas_call(functools.partial(kernel, lines, planes, cores, logit_scal...  28.8 us
    unnamed x8, local copies, waits for them, and re-layouts  3.48 us

profile of v1, /device:TPU:0, one launch (start us, length us, event | category | flops | bytes accessed | tf_op | source)
XLA Modules:
  0.0 32.9 jit_solution(18131115825212909520)
XLA Ops:
  0.6 0.0 copy-start.2
  0.6 0.6 %copy-done.2 = s32[128]{0:T(128)S(1)} copy-done((s32[128]{0:T(128)S(1)}, s32[128]{0:T(128)}, u32[]{:S(2)}) %copy-start.2) | copy-done | bytes 536
  1.3 0.0 copy-start
  1.3 0.8 %copy-done = f32[128,128]{1,0:T(8,128)S(1)} copy-done((f32[128,128]{1,0:T(8,128)S(1)}, f32[128,128]{1,0:T(8,128)}, u32[]{:S(2)}) %copy-start) | copy-done | bytes 65560
  2.1 0.0 copy-start.1
  2.1 0.8 %copy-done.1 = f32[128,64]{0,1:T(8,128)S(1)} copy-done((f32[128,64]{0,1:T(8,128)S(1)}, f32[128,64]{0,1:T(8,128)}, u32[]{:S(2)}) %copy-start.1) | copy-done | bytes 32792
  2.9 28.8 %shard_map.50 = (f32[64,128]{1,0:T(8,128)S(1)}, f32[64,128]{1,0:T(8,128)S(1)}) custom-call(f32[128,128]{1,0:T(8,128)S(1)} %copy-done, s32[1,128]{1,0:T(1,128)S(1)} %bitcast.7, f32[64,128]{1,0:T(8,128)S(1)} %bitcast.4), custom_call_target="tpu_custom_call" | custom-call | tf_op jit(solution)/shard_map/pallas_call | solution.py:174
  31.7 0.6 %copy.7 = f32[128,64]{0,1:T(8,128)} copy(f32[128,64]{0,1:T(8,128)S(1)} %bitcast.6) | data formatting | bytes 65536
  32.3 0.6 %copy.8 = f32[128,64]{0,1:T(8,128)} copy(f32[128,64]{0,1:T(8,128)S(1)} %bitcast.5) | data formatting | bytes 65536
Async XLA Ops:
  0.6 0.7 %copy-start.2 = (s32[128]{0:T(128)S(1)}, s32[128]{0:T(128)}, u32[]{:S(2)}) copy-start(s32[128]{0:T(128)} %param.4) | copy-start | bytes 1540
  1.3 0.8 %copy-start = (f32[128,128]{1,0:T(8,128)S(1)}, f32[128,128]{1,0:T(8,128)}, u32[]{:S(2)}) copy-start(f32[128,128]{1,0:T(8,128)} %points_ref.1) | copy-start | bytes 196612
  2.1 0.8 %copy-start.1 = (f32[128,64]{0,1:T(8,128)S(1)}, f32[128,64]{0,1:T(8,128)}, u32[]{:S(2)}) copy-start(f32[128,64]{0,1:T(8,128)} %param.5) | copy-start | bytes 98308

commit v2 on v1

--- a/solution.py
+++ b/solution.py
@@ -12,6 +12,10 @@
 NT = (((1,), (1,)), ((), ()))
 NN = (((1,), (0,)), ((), ()))
 GATHER_PLANE = False
+LINE_ORDER = (2, 3, 1)
+PLANE_ORDER = (6, 7, 2, 4, 3, 5, 1)
+VALUE_ORDER = (2, 3, 1)
+SUM_ORDER = (6, 7, 2, 4, 3, 5, 1)
 
 
 def split_bf16(x):
@@ -20,12 +24,28 @@
     return hi, lo
 
 
+def peer(i, k, n):
+    if n & (n - 1):
+        return lax.rem(i + k, n)
+    out = 0
+    bit = 1
+    while bit < n:
+        out += ((i // bit + k // bit) % 2) * bit
+        bit *= 2
+    return out
+
+
+def order(n, first):
+    return [k for k in first if k < n] + [k for k in range(1, n) if k not in first]
+
+
 def kernel(
     lines, planes, cores, logit_scale,
+    points_hbm, labels_hbm, coef_hbm,
+    out_ref,
     points_ref, labels_ref, coef_ref,
-    new_ref, prob_ref,
     line_pts, plane_pts, values, tile, partial, landed,
-    line_send, line_recv, plane_send, plane_recv, value_send, value_recv, part_send, part_recv,
+    line_send, line_recv, plane_send, plane_recv, value_send, value_recv, part_send, part_recv, input_sem,
 ):
     own, feat = points_ref.shape
     classes = coef_ref.shape[0]
@@ -47,21 +67,32 @@
         gathers, my_gather, gather_device, gather_pts = lines, my_line, line_device, line_pts
         reduces, my_reduce, reduce_device, reduce_pts = planes, my_plane, plane_device, plane_pts
 
+    loads = [
+        pltpu.make_async_copy(src, dst, input_sem.at[i])
+        for i, (src, dst) in enumerate(
+            [(points_hbm, points_ref), (coef_hbm, coef_ref), (labels_hbm, labels_ref)]
+        )
+    ]
+    for load in loads:
+        load.start()
     barrier = pltpu.get_barrier_semaphore()
     for k in range(1, lines):
         pl.semaphore_signal(
-            barrier, inc=1, device_id=line_device(lax.rem(my_line + k, lines)), device_id_type=MESH
+            barrier, inc=1, device_id=line_device(peer(my_line, k, lines)), device_id_type=MESH
         )
     for k in range(1, planes):
         pl.semaphore_signal(
-            barrier, inc=1, device_id=plane_device(lax.rem(my_plane + k, planes)), device_id_type=MESH
-        )
-
+            barrier, inc=1, device_id=plane_device(peer(my_plane, k, planes)), device_id_type=MESH
+        )
+
+    loads[0].wait()
     hi, lo = split_bf16(points_ref[...])
     line_pts[my_line, :, :feat] = hi
     line_pts[my_line, :, feat:] = lo
     plane_pts[my_plane, :, :feat] = hi
     plane_pts[my_plane, :, feat:] = lo
+    loads[1].wait()
+    loads[2].wait()
     values[0, my_gather] = coef_ref[...].astype(jnp.bfloat16)
     pl.semaphore_wait(barrier, lines + planes - 2)
 
@@ -76,16 +107,16 @@
         pltpu.make_async_copy(buf, buf, sem).wait()
 
     sent = []
-    for k in range(1, lines):
-        to = lax.rem(my_line + k, lines)
+    for k in order(lines, LINE_ORDER):
+        to = peer(my_line, k, lines)
         sent.append(push(line_pts.at[my_line], line_pts.at[my_line], line_send.at[k], line_recv.at[my_line], line_device(to)))
-    for k in range(1, planes):
-        to = lax.rem(my_plane + k, planes)
+    for k in order(planes, PLANE_ORDER):
+        to = peer(my_plane, k, planes)
         sent.append(push(plane_pts.at[my_plane], plane_pts.at[my_plane], plane_send.at[k], plane_recv.at[my_plane], plane_device(to)))
 
     def send_values(phase):
-        for k in range(1, gathers):
-            to = lax.rem(my_gather + k, gathers)
+        for k in order(gathers, VALUE_ORDER):
+            to = peer(my_gather, k, gathers)
             sent.append(push(
                 values.at[phase, my_gather], values.at[phase, my_gather],
                 value_send.at[phase, k], value_recv.at[phase, my_gather], gather_device(to),
@@ -94,7 +125,7 @@
     send_values(0)
 
     def wait_block(group, buf, recv, me, count, k):
-        at = lax.rem(me + count - k, count)
+        at = peer(me, k, count)
         recv_wait(buf.at[at], recv.at[at])
         return at
 
@@ -127,7 +158,7 @@
 
     def apply(phase):
         for k in range(1, gathers):
-            at = lax.rem(my_gather + gathers - k, gathers)
+            at = peer(my_gather, k, gathers)
             recv_wait(values.at[phase, at], value_recv.at[phase, at])
         left = jnp.concatenate([values[phase, i] for i in range(gathers)], axis=1)
         result = lax.dot_general(
@@ -135,15 +166,15 @@
         )
         for j in range(reduces):
             partial[phase, j] = result[:, j * own : (j + 1) * own]
-        for k in range(1, reduces):
-            to = lax.rem(my_reduce + k, reduces)
+        for k in order(reduces, SUM_ORDER):
+            to = peer(my_reduce, k, reduces)
             sent.append(push(
                 partial.at[phase, to], landed.at[phase, my_reduce],
                 part_send.at[phase, k], part_recv.at[phase, my_reduce], reduce_device(to),
             ))
         total = partial[phase, my_reduce]
         for k in range(1, reduces):
-            at = lax.rem(my_reduce + reduces - k, reduces)
+            at = peer(my_reduce, k, reduces)
             recv_wait(landed.at[phase, at], part_recv.at[phase, at])
             total += landed[phase, at]
         return total
@@ -154,8 +185,8 @@
     onehot = (lax.broadcasted_iota(jnp.int32, (classes, own), 0) == labels_ref[...]).astype(jnp.float32)
     values[1, my_gather] = (logit_scale * (probabilities - onehot)).astype(jnp.bfloat16)
     send_values(1)
-    prob_ref[...] = probabilities
-    new_ref[...] = coef_ref[...] - apply(1)
+    out_ref[1] = -probabilities
+    out_ref[0] = apply(1) - coef_ref[...]
     for copy in sent:
         copy.wait_send()
 
@@ -171,12 +202,15 @@
         classes = coefficients.shape[1]
         logit_scale = 16.0 / math.sqrt(own * rows * cols)
         vmem = pl.BlockSpec(memory_space=pltpu.VMEM)
-        new, prob = pl.pallas_call(
+        negated = pl.pallas_call(
             functools.partial(kernel, lines, planes, cores, logit_scale),
-            out_shape=[jax.ShapeDtypeStruct((classes, own), jnp.float32)] * 2,
-            in_specs=[vmem] * 3,
-            out_specs=[vmem] * 2,
+            out_shape=jax.ShapeDtypeStruct((2, classes, own), jnp.float32),
+            in_specs=[pl.BlockSpec(memory_space=pltpu.MemorySpace.HBM)] * 3,
+            out_specs=vmem,
             scratch_shapes=[
+                pltpu.VMEM((own, feat), jnp.float32),
+                pltpu.VMEM((1, own), jnp.int32),
+                pltpu.VMEM((classes, own), jnp.float32),
                 pltpu.VMEM((lines, own, 2 * feat), jnp.bfloat16),
                 pltpu.VMEM((planes, own, 2 * feat), jnp.bfloat16),
                 pltpu.VMEM((2, gathers, classes, own), jnp.bfloat16),
@@ -191,12 +225,13 @@
                 pltpu.SemaphoreType.DMA((2, gathers)),
                 pltpu.SemaphoreType.DMA((2, reduces)),
                 pltpu.SemaphoreType.DMA((2, reduces)),
+                pltpu.SemaphoreType.DMA((3,)),
             ],
             compiler_params=pltpu.CompilerParams(
                 collective_id=0, has_side_effects=True, vmem_limit_bytes=48 * 1024 * 1024
             ),
-        )(points, labels.reshape(1, own), coefficients.T)
-        return new.T, prob.T
+        )(*[pltpu.with_memory_space_constraint(x, pltpu.MemorySpace.HBM) for x in (points, labels.reshape(1, own), coefficients.T)])
+        return -negated[0].T, -negated[1].T
 
     return jax.shard_map(
         on_device,

time: 33.1 us -> 30.2 us (0.912)
  local copies, waits for them, and re-layouts: 3.48 us -> 0 us
  other arithmetic: 0 us -> 0.63 us
    unnamed x8 -> x0, local copies, waits for them, and re-layouts: 3.48 us -> none
    neg x0 -> x1, other arithmetic: none -> 0.63 us  [on_device(): return (-negated[0].T, -negated[1].T)]
where the time goes in v2:
time: 30.2 us; the launch traced here: 30 us
  Pallas kernels  28.8 us (95%)
  between operations  0.64 us (2%)
  other arithmetic  0.63 us (2%)
    pallas_call x1, Pallas kernels, on_device(): pl.pallas_call(functools.partial(kernel, lines, planes, cores, logit_scal...  28.8 us
    neg x1, other arithmetic, on_device(): return (-negated[0].T, -negated[1].T)  0.63 us

profile of v2, /device:TPU:0, one launch (start us, length us, event | category | flops | bytes accessed | tf_op | source)
XLA Modules:
  0.0 30.0 jit_solution(5169060767760471264)
XLA Ops:
  0.6 28.8 %shard_map.50 = f32[2,64,128]{2,1,0:T(8,128)S(1)} custom-call(f32[128,128]{1,0:T(8,128)} %points_hbm.1, s32[1,128]{1,0:T(1,128)} %bitcast.11, f32[64,128]{1,0:T(8,128)} %bitcast.10), custom_call_target="tpu_custom_call" | custom-call | tf_op jit(solution)/shard_map/pallas_call | solution.py:205
  29.4 0.6 %negate_bitcast_fusion = (f32[128,64]{0,1:T(8,128)}, f32[128,64]{0,1:T(8,128)}) fusion(f32[2,64,128]{2,1,0:T(8,128)S(1)} %shard_map.50), kind=kLoop, calls=%fused_computation | loop fusion | flops 16384 | bytes 131072 | tf_op jit(solution)/shard_map/neg | solution.py:234

commit v3 on v2

--- a/solution.py
+++ b/solution.py
@@ -13,6 +13,7 @@
 NN = (((1,), (0,)), ((), ()))
 GATHER_PLANE = False
 LINE_ORDER = (2, 3, 1)
+TILE_ORDER = (0, 2, 1, 3)
 PLANE_ORDER = (6, 7, 2, 4, 3, 5, 1)
 VALUE_ORDER = (2, 3, 1)
 SUM_ORDER = (6, 7, 2, 4, 3, 5, 1)
@@ -73,10 +74,8 @@
             [(points_hbm, points_ref), (coef_hbm, coef_ref), (labels_hbm, labels_ref)]
         )
     ]
-    for load in loads:
-        load.start()
     barrier = pltpu.get_barrier_semaphore()
-    for k in range(1, lines):
+    for k in range(lines - 1, 0, -1):
         pl.semaphore_signal(
             barrier, inc=1, device_id=line_device(peer(my_line, k, lines)), device_id_type=MESH
         )
@@ -85,6 +84,8 @@
             barrier, inc=1, device_id=plane_device(peer(my_plane, k, planes)), device_id_type=MESH
         )
 
+    for load in loads:
+        load.start()
     loads[0].wait()
     hi, lo = split_bf16(points_ref[...])
     line_pts[my_line, :, :feat] = hi
@@ -107,9 +108,26 @@
         pltpu.make_async_copy(buf, buf, sem).wait()
 
     sent = []
+    relay = lines == 4
+    middle = (my_line == 1) | (my_line == 2)
+
+    def line_push(src, k):
+        to = peer(my_line, k, lines)
+        return pltpu.make_async_remote_copy(
+            src_ref=line_pts.at[src], dst_ref=line_pts.at[src],
+            send_sem=line_send.at[k], recv_sem=line_recv.at[src],
+            device_id=line_device(to), device_id_type=MESH,
+        )
+
     for k in order(lines, LINE_ORDER):
-        to = peer(my_line, k, lines)
-        sent.append(push(line_pts.at[my_line], line_pts.at[my_line], line_send.at[k], line_recv.at[my_line], line_device(to)))
+        if relay and k == 3:
+            @pl.when(middle)
+            def _():
+                line_push(my_line, 3).start()
+        else:
+            copy = line_push(my_line, k)
+            copy.start()
+            sent.append(copy)
     for k in order(planes, PLANE_ORDER):
         to = peer(my_plane, k, planes)
         sent.append(push(plane_pts.at[my_plane], plane_pts.at[my_plane], plane_send.at[k], plane_recv.at[my_plane], plane_device(to)))
@@ -128,6 +146,18 @@
         at = peer(me, k, count)
         recv_wait(buf.at[at], recv.at[at])
         return at
+
+    if relay:
+        far = peer(my_line, 2, lines)
+        recv_wait(line_pts.at[far], line_recv.at[far])
+
+        @pl.when(middle)
+        def _():
+            pltpu.make_async_remote_copy(
+                src_ref=line_pts.at[far], dst_ref=line_pts.at[far],
+                send_sem=line_send.at[0], recv_sem=line_recv.at[far],
+                device_id=line_device(peer(my_line, 1, lines)), device_id_type=MESH,
+            ).start()
 
     reduce_recv = line_recv if GATHER_PLANE else plane_recv
     gather_recv = plane_recv if GATHER_PLANE else line_recv
@@ -141,11 +171,13 @@
         preferred_element_type=jnp.float32,
     )[:1]
 
-    for k in range(gathers):
+    for k in TILE_ORDER if gathers == 4 else range(gathers):
         if k == 0:
             at = my_gather
         else:
-            at = wait_block("gather", gather_pts, gather_recv, my_gather, gathers, k)
+            at = peer(my_gather, k, gathers)
+            if not (relay and not GATHER_PLANE and k == 2):
+                recv_wait(gather_pts.at[at], gather_recv.at[at])
         left = gather_pts[at]
         left_hi, left_lo = left[:, :feat], left[:, feat:]
         left_f32 = left_hi.astype(jnp.float32) + left_lo.astype(jnp.float32)
@@ -189,6 +221,15 @@
     out_ref[0] = apply(1) - coef_ref[...]
     for copy in sent:
         copy.wait_send()
+    if relay:
+        @pl.when(middle)
+        def _():
+            line_push(my_line, 3).wait_send()
+            pltpu.make_async_remote_copy(
+                src_ref=line_pts.at[far], dst_ref=line_pts.at[far],
+                send_sem=line_send.at[0], recv_sem=line_recv.at[far],
+                device_id=line_device(peer(my_line, 1, lines)), device_id_type=MESH,
+            ).wait_send()
 
 
 def solution(mesh):

time: 30.2 us -> 29.9 us (0.990)
  Pallas kernels: 28.8 us -> 28.4 us
    pallas_call x1, Pallas kernels: 28.8 us -> 28.4 us  [on_device(): pl.pallas_call(functools.partial(kernel, lines, planes, cores, logit_scal...]
where the time goes in v3:
time: 29.9 us; the launch traced here: 29.7 us
  Pallas kernels  28.4 us (95%)
  between operations  0.64 us (2%)
  other arithmetic  0.63 us (2%)
    pallas_call x1, Pallas kernels, on_device(): pl.pallas_call(functools.partial(kernel, lines, planes, cores, logit_scal...  28.4 us
    neg x1, other arithmetic, on_device(): return (-negated[0].T, -negated[1].T)  0.63 us

profile of v3, /device:TPU:0, one launch (start us, length us, event | category | flops | bytes accessed | tf_op | source)
XLA Modules:
  0.0 29.7 jit_solution(8617151389061664972)
XLA Ops:
  0.6 28.4 %shard_map.50 = f32[2,64,128]{2,1,0:T(8,128)S(1)} custom-call(f32[128,128]{1,0:T(8,128)} %points_hbm.1, s32[1,128]{1,0:T(1,128)} %bitcast.11, f32[64,128]{1,0:T(8,128)} %bitcast.10), custom_call_target="tpu_custom_call" | custom-call | tf_op jit(solution)/shard_map/pallas_call | solution.py:246
  29.1 0.6 %negate_bitcast_fusion = (f32[128,64]{0,1:T(8,128)}, f32[128,64]{0,1:T(8,128)}) fusion(f32[2,64,128]{2,1,0:T(8,128)S(1)} %shard_map.50), kind=kLoop, calls=%fused_computation | loop fusion | flops 16384 | bytes 131072 | tf_op jit(solution)/shard_map/neg | solution.py:275

commit v4 on v3

--- a/solution.py
+++ b/solution.py
@@ -15,7 +15,7 @@
 LINE_ORDER = (2, 3, 1)
 TILE_ORDER = (0, 2, 1, 3)
 PLANE_ORDER = (6, 7, 2, 4, 3, 5, 1)
-VALUE_ORDER = (2, 3, 1)
+VALUE_ORDER = (3, 2, 1)
 SUM_ORDER = (6, 7, 2, 4, 3, 5, 1)
 
 
@@ -128,10 +128,6 @@
             copy = line_push(my_line, k)
             copy.start()
             sent.append(copy)
-    for k in order(planes, PLANE_ORDER):
-        to = peer(my_plane, k, planes)
-        sent.append(push(plane_pts.at[my_plane], plane_pts.at[my_plane], plane_send.at[k], plane_recv.at[my_plane], plane_device(to)))
-
     def send_values(phase):
         for k in order(gathers, VALUE_ORDER):
             to = peer(my_gather, k, gathers)
@@ -141,6 +137,10 @@
             ))
 
     send_values(0)
+
+    for k in order(planes, PLANE_ORDER):
+        to = peer(my_plane, k, planes)
+        sent.append(push(plane_pts.at[my_plane], plane_pts.at[my_plane], plane_send.at[k], plane_recv.at[my_plane], plane_device(to)))
 
     def wait_block(group, buf, recv, me, count, k):
         at = peer(me, k, count)

time: 29.9 us -> 29.7 us (level)
  no operation moved by 1% of the time
where the time goes in v4:
time: 29.7 us; the launch traced here: 29.6 us
  Pallas kernels  28.3 us (95%)
  between operations  0.64 us (2%)
  other arithmetic  0.63 us (2%)
    pallas_call x1, Pallas kernels, on_device(): pl.pallas_call(functools.partial(kernel, lines, planes, cores, logit_scal...  28.3 us
    neg x1, other arithmetic, on_device(): return (-negated[0].T, -negated[1].T)  0.63 us

profile of v4, /device:TPU:0, one launch (start us, length us, event | category | flops | bytes accessed | tf_op | source)
XLA Modules:
  0.0 29.6 jit_solution(4181393257791415265)
XLA Ops:
  0.6 28.3 %shard_map.50 = f32[2,64,128]{2,1,0:T(8,128)S(1)} custom-call(f32[128,128]{1,0:T(8,128)} %points_hbm.1, s32[1,128]{1,0:T(1,128)} %bitcast.11, f32[64,128]{1,0:T(8,128)} %bitcast.10), custom_call_target="tpu_custom_call" | custom-call | tf_op jit(solution)/shard_map/pallas_call | solution.py:246
  28.9 0.6 %negate_bitcast_fusion = (f32[128,64]{0,1:T(8,128)}, f32[128,64]{0,1:T(8,128)}) fusion(f32[2,64,128]{2,1,0:T(8,128)S(1)} %shard_map.50), kind=kLoop, calls=%fused_computation | loop fusion | flops 16384 | bytes 131072 | tf_op jit(solution)/shard_map/neg | solution.py:275
